TPU v7x, 32 devices: a whole 2x2x4 slice. The times are simulated.
32 devices in a mesh: enc: 4 (over z), grp: 8 (over y, x, core).
Axes of the slice: x: 2, y: 2, z: 4, core: 2. Of those that a mesh axis runs over, the one named last changes fastest.
Arguments:
- query_raw: bfloat16 [6144, 1024], P(('enc', 'grp')), may hold values from -6 to 6
- key_raw: bfloat16 [6144, 1024], P(('enc', 'grp')), may hold values from -6 to 6
- value_rows: bfloat16 [6144, 1024], P(('enc', 'grp')), may hold values from -6 to 6
- out_cotangent: bfloat16 [6144, 1024], P(('enc', 'grp')), may hold values from -6 to 6
- image_ids: int32 [6144], P(('enc', 'grp')), may hold values from 0 to 15, as said below
- owners: int32 [8, 4, 12], P('grp'), may hold values from -1 to 3, as said below
- gains: float32 [2, 1024], replicated, may hold values from 0.1 to 1.9
Outputs:
- query_grad: bfloat16 [4096, 1024], P(('enc', 'grp'))
- key_grad: bfloat16 [4096, 1024], P(('enc', 'grp'))
- value_grad: bfloat16 [4096, 1024], P(('enc', 'grp'))
- gain_grad: float32 [2, 1024], P(None, 'grp')
Inputs may be any that keep to these rules, and one draw needn't show every extreme that they name: `image_ids`: inside each piece of 16 rows the number is 0 at the first row and rises by 0 or 1 from row to row. `owners`: A loader's live slots come first; a loader gives at most 3 pieces to one owner and some loader of each group gives exactly 3 to every owner; every owner receives exactly 8 pieces of its group.
All inputs are finite; a program needn't handle non-finite values.
Results may differ from a plain program's by a relative error of at most 0.0073.
Values may be sent and summed in bfloat16 or wider, within the bound.
A program may use at most 64 MiB of HBM per device.

v0:
```python
import math

import jax
import jax.numpy as jnp
from jax import lax
from jax.sharding import PartitionSpec as P

HEADS = 16
HD = 64
PIECE = 16
PMAX = 12
P_OWN = 8


epsilon = 1e-05


def normalize(blocks, gain_row):
    num_pieces = blocks.shape[0]
    values_four = blocks.astype(jnp.float32).reshape(num_pieces, PIECE, HEADS, HD)
    centred = values_four - jnp.mean(values_four, -1, keepdims=True)
    inv_scale = lax.rsqrt(jnp.mean(centred * centred, -1, keepdims=True) + epsilon)
    normed = centred * inv_scale
    return (normed, inv_scale, (normed * gain_row).astype(jnp.bfloat16))


def norm_back(d_hat, normed, inv_scale, gain_row, live_flags):
    d_norm = d_hat * gain_row
    d_input = inv_scale * (
        d_norm
        - jnp.mean(d_norm, -1, keepdims=True)
        - normed * jnp.mean(d_norm * normed, -1, keepdims=True)
    )
    gain_term = jnp.sum(d_hat * normed * live_flags[:, None, None, None], (0, 1))
    return (d_input, gain_term.reshape(-1))


def piece_grads(query_rows, key_rows, value_rows, cotangent, image_num, gains, live_flags):
    num_pieces = query_rows.shape[0]
    four_shape = (num_pieces, PIECE, HEADS, HD)
    gain_query = gains[0].reshape(HEADS, HD)
    gain_key = gains[1].reshape(HEADS, HD)
    q_norm, q_scale, q_hat = normalize(query_rows, gain_query)
    k_norm, k_scale, k_hat = normalize(key_rows, gain_key)
    values_four = value_rows.reshape(four_shape)
    cot_four = cotangent.reshape(four_shape)
    factor = HD ** (-0.5)
    scores = (
        jnp.einsum("bihd,bjhd->bhij", q_hat, k_hat, preferred_element_type=jnp.float32) * factor
    )
    same_image = image_num[:, None, :, None] == image_num[:, None, None, :]
    weights = jnp.where(same_image, jnp.exp(scores), 0.0)
    probs = weights / jnp.sum(weights, -1, keepdims=True)
    probs_b = probs.astype(jnp.bfloat16)
    attended = jnp.einsum(
        "bhij,bjhd->bihd", probs_b, values_four, preferred_element_type=jnp.float32
    )
    row_delta = jnp.sum(cot_four.astype(jnp.float32) * attended, -1)
    d_value = jnp.einsum(
        "bhij,bihd->bjhd", probs_b, cot_four, preferred_element_type=jnp.float32
    ).astype(jnp.bfloat16)
    d_prob = jnp.einsum(
        "bihd,bjhd->bhij", cot_four, values_four, preferred_element_type=jnp.float32
    )
    d_score = (probs * (d_prob - jnp.transpose(row_delta, (0, 2, 1))[..., None]) * factor).astype(
        jnp.bfloat16
    )
    d_qhat = jnp.einsum("bhij,bjhd->bihd", d_score, k_hat, preferred_element_type=jnp.float32)
    d_khat = jnp.einsum("bhij,bihd->bjhd", d_score, q_hat, preferred_element_type=jnp.float32)
    d_query, term_query = norm_back(d_qhat, q_norm, q_scale, gain_query, live_flags)
    d_key, term_key = norm_back(d_khat, k_norm, k_scale, gain_key, live_flags)
    flat_shape = (num_pieces, PIECE, HEADS * HD)
    return (
        d_query.reshape(flat_shape).astype(jnp.bfloat16),
        d_key.reshape(flat_shape).astype(jnp.bfloat16),
        d_value.reshape(flat_shape),
        jnp.stack([term_query, term_key]),
    )


def send_slots(own_plan, enc_count, per_slot):
    owner_hit = (own_plan[:, None] == jnp.arange(enc_count, dtype=jnp.int32)[None, :]).astype(
        jnp.int32
    )
    slot_rank = jnp.sum((jnp.cumsum(owner_hit, 0) - owner_hit) * owner_hit, 1)
    slot_target = jnp.where(own_plan >= 0, own_plan * per_slot + slot_rank, -1)
    slot_ids = jnp.arange(enc_count * per_slot, dtype=jnp.int32)
    matches = (slot_target[None, :] == slot_ids[:, None]).astype(jnp.int32)
    slot_source = jnp.sum(matches * jnp.arange(PMAX, dtype=jnp.int32)[None, :], 1)
    slot_filled = jnp.sum(matches, 1) > 0
    return (slot_source, slot_filled)


def receive_order(group_plan, enc_rank, enc_count, per_slot):
    arrived = jnp.sum((group_plan == enc_rank).astype(jnp.int32), 1)
    live_slots = (
        (jnp.arange(per_slot, dtype=jnp.int32)[None, :] < arrived[:, None])
        .reshape(-1)
        .astype(jnp.int32)
    )
    live_order = jnp.cumsum(live_slots) - 1
    wanted = jnp.arange(P_OWN, dtype=jnp.int32)
    matches = ((live_order[None, :] == wanted[:, None]) & (live_slots[None, :] > 0)).astype(
        jnp.int32
    )
    return jnp.sum(matches * jnp.arange(enc_count * per_slot, dtype=jnp.int32)[None, :], 1)


def to_slots(pieces, slot_source, slot_filled, enc_count):
    taken = jnp.take(pieces, slot_source, axis=0)
    mask_shape = (slot_filled.shape[0],) + (1,) * (pieces.ndim - 1)
    taken = jnp.where(slot_filled.reshape(mask_shape), taken, jnp.zeros_like(taken))
    return taken.reshape((enc_count, -1) + pieces.shape[2:])


def from_slots(received, arrival_order):
    flat_pieces = received.reshape((-1, PIECE) + received.shape[2:])
    return jnp.take(flat_pieces, arrival_order, axis=0)


def local(query_raw, key_raw, value_rows, out_cotangent, image_ids, owners, gains):
    enc_count = lax.axis_size("enc")
    enc_rank = lax.axis_index("enc")
    per_slot = PMAX // enc_count
    feat = HEADS * HD
    group_plan = owners[0]
    own_plan = lax.dynamic_index_in_dim(group_plan, enc_rank, 0, keepdims=False)
    slot_source, slot_filled = send_slots(own_plan, enc_count, per_slot)
    arrival_order = receive_order(group_plan, enc_rank, enc_count, per_slot)
    piece_shape = (PMAX, PIECE, feat)
    packed = tuple(
        (
            to_slots(array.reshape(piece_shape), slot_source, slot_filled, enc_count)
            for array in (query_raw, key_raw, value_rows, out_cotangent)
        )
    )
    image_slots = to_slots(
        image_ids.astype(jnp.bfloat16).reshape(PMAX, PIECE), slot_source, slot_filled, enc_count
    )
    received = (
        lax.all_to_all(packed[0], "enc", split_axis=0, concat_axis=0, tiled=True),
        lax.all_to_all(packed[1], "enc", split_axis=0, concat_axis=0, tiled=True),
        lax.all_to_all(packed[2], "enc", split_axis=0, concat_axis=0, tiled=True),
        lax.all_to_all(packed[3], "enc", split_axis=0, concat_axis=0, tiled=True),
        lax.all_to_all(image_slots, "enc", split_axis=0, concat_axis=0, tiled=True),
    )
    mine_q, mine_k, mine_v, mine_d, mine_i = (
        from_slots(array, arrival_order) for array in received
    )
    d_query, d_key, d_value, gain_terms = piece_grads(
        mine_q, mine_k, mine_v, mine_d, mine_i, gains, jnp.ones((P_OWN,), jnp.float32)
    )
    group_total = lax.psum(gain_terms, "enc")
    shares = lax.psum_scatter(group_total, "grp", scatter_dimension=1, tiled=True)
    total_live = enc_count * lax.axis_size("grp") * P_OWN * PIECE
    gain_grad = shares / math.sqrt(total_live)
    own_rows = P_OWN * PIECE
    return (
        d_query.reshape(own_rows, feat),
        d_key.reshape(own_rows, feat),
        d_value.reshape(own_rows, feat),
        gain_grad,
    )


def solution(mesh):
    return jax.shard_map(
        local,
        mesh=mesh,
        in_specs=(
            P(("enc", "grp"), None),
            P(("enc", "grp"), None),
            P(("enc", "grp"), None),
            P(("enc", "grp"), None),
            P(("enc", "grp")),
            P("grp", None, None),
            P(),
        ),
        out_specs=(
            P(("enc", "grp"), None),
            P(("enc", "grp"), None),
            P(("enc", "grp"), None),
            P(None, "grp"),
        ),
        check_vma=False,
    )
```

profile of v0, /device:TPU:0, one launch (start us, length us, event | category | flops | bytes accessed | tf_op | source)
XLA Modules:
  0.0 177.1 jit_solution(3159887669811033840)
XLA Ops:
  7.2 0.7 copy-done.21
  8.4 0.6 copy-done.22
  10.2 0.6 copy.107
  10.8 6.3 %all-to-all-start.2 = ((bf16[4,1,48]{2,1,0:T(2,128)(2,1)}), bf16[4,1,48]{2,1,0:T(2,128)(2,1)S(1)}, u32[]{:S(2)}, u32[]{:S(2)}) async-start(bf16[4,1,48]{2,1,0:T(2,128)(2,1)} %copy.107), calls=%async_computation.2 | async-start | bytes 4096 | tf_op jit(solution)/shard_map/all_to_all | solution.py:145
  20.7 1.2 select_select_fusion.1
  21.8 0.7 all-to-all-done.2
  22.5 15.3 %all_to_all.26 = bf16[4,48,1024]{2,1,0:T(8,128)(2,1)S(1)} all-to-all(bf16[4,48,1024]{2,1,0:T(8,128)(2,1)S(1)} %bitcast.51), channel_id=1, replica_groups=mesh['enc'=4,'grp'=8] {'enc'}, dimensions={0} | all-to-all | bytes 786432 | tf_op jit(solution)/shard_map/all_to_all | solution.py:142
  37.8 3.5 %all-to-all-start.3 = ((bf16[4,48,1024]{2,1,0:T(8,128)(2,1)}), bf16[4,48,1024]{2,1,0:T(8,128)(2,1)S(1)}, u32[]{:S(2)}, u32[]{:S(2)}) async-start(bf16[4,48,1024]{2,1,0:T(8,128)(2,1)} %bitcast.13), calls=%async_computation.3 | async-start | bytes 786432 | tf_op jit(solution)/shard_map/all_to_all | solution.py:144
  42.0 9.8 %all-to-all-done.3 = bf16[4,48,1024]{2,1,0:T(8,128)(2,1)S(1)} async-done(((bf16[4,48,1024]{2,1,0:T(8,128)(2,1)}), bf16[4,48,1024]{2,1,0:T(8,128)(2,1)S(1)}, u32[]{:S(2)}, u32[]{:S(2)}) %all-to-all-start.3) | async-done | bytes 393248 | tf_op jit(solution)/shard_map/all_to_all | solution.py:144
  51.8 3.6 %all-to-all-start.4 = ((bf16[4,48,1024]{2,1,0:T(8,128)(2,1)}), bf16[4,48,1024]{2,1,0:T(8,128)(2,1)S(1)}, u32[]{:S(2)}, u32[]{:S(2)}) async-start(bf16[4,48,1024]{2,1,0:T(8,128)(2,1)} %bitcast.16), calls=%async_computation.4 | async-start | bytes 786432 | tf_op jit(solution)/shard_map/all_to_all | solution.py:143
  55.5 9.8 %all-to-all-done.4 = bf16[4,48,1024]{2,1,0:T(8,128)(2,1)S(1)} async-done(((bf16[4,48,1024]{2,1,0:T(8,128)(2,1)}), bf16[4,48,1024]{2,1,0:T(8,128)(2,1)S(1)}, u32[]{:S(2)}, u32[]{:S(2)}) %all-to-all-start.4) | async-done | bytes 393248 | tf_op jit(solution)/shard_map/all_to_all | solution.py:143
  65.2 3.5 %all-to-all-start = ((bf16[4,48,1024]{2,1,0:T(8,128)(2,1)}), bf16[4,48,1024]{2,1,0:T(8,128)(2,1)S(1)}, u32[]{:S(2)}, u32[]{:S(2)}) async-start(bf16[4,48,1024]{2,1,0:T(8,128)(2,1)} %bitcast.3), calls=%async_computation | async-start | bytes 786432 | tf_op jit(solution)/shard_map/all_to_all | solution.py:141
  69.7 0.7 broadcast_compare_fusion
  72.1 6.4 %all-to-all-done = bf16[4,48,1024]{2,1,0:T(8,128)(2,1)S(1)} async-done(((bf16[4,48,1024]{2,1,0:T(8,128)(2,1)}), bf16[4,48,1024]{2,1,0:T(8,128)(2,1)S(1)}, u32[]{:S(2)}, u32[]{:S(2)}) %all-to-all-start) | async-done | bytes 393248 | tf_op jit(solution)/shard_map/all_to_all | solution.py:141
  79.2 1.1 reshape.354
  80.3 1.1 reshape.358
  82.2 0.8 multiply_reduce_fusion.4
  83.1 0.7 copy.106
  84.5 0.8 multiply_reduce_fusion.5
  85.4 0.7 copy.102
  86.1 2.2 %fusion.11 = f32[8,16,16,16]{2,3,1,0:T(8,128)S(1)} fusion(pred[8,16,16]{1,2,0:T(8,128)(4,1)} %broadcast_compare_fusion, f32[16,64]{1,0:T(8,128)S(1)} %mul.143, f32[8,16,16]{1,2,0:T(8,128)} %copy.106, f32[8,16,16]{1,2,0:T(8,128)} %copy-done.7, f32[8,16,16,64]{3,2,1,0:T(8,128)S(1)} %reshape.363, f32[16,64]{1,0:T(8,128)S(1)} %mul.147, ...), kind=kOutput, calls=%fused_computation.41 | convolution fusion | flops 5343247 | bytes 1222656 | tf_op jit(solution)/shard_map/div | solution.py:53
  88.4 1.8 %fusion.6 = f32[8,16,16]{1,2,0:T(8,128)S(1)} fusion(bf16[8,16,16,64]{3,2,1,0:T(8,128)(2,1)} %reshape.358, bf16[8,16,16,64]{3,2,1,0:T(8,128)(2,1)} %reshape.354, f32[8,16,16,16]{2,3,1,0:T(8,128)S(1)} %fusion.11), kind=kOutput, calls=%fused_computation.22 | convolution fusion | flops 4618240 | bytes 663552 | tf_op jit(solution)/shard_map/bhij,bjhd->bihd/dot_general | solution.py:55
  91.2 4.0 %multiply_reduce_fusion = (f32[16,64]{1,0:T(8,128)}, f32[8,16,16]{1,2,0:T(8,128)}, f32[8,16,16]{1,2,0:T(8,128)}, f32[8,16,16,64]{3,1,2,0:T(8,128)}) fusion(f32[8,16,16]{1,2,0:T(8,128)S(1)} %copy-done.15, f32[8,16,16]{1,2,0:T(8,128)S(1)} %copy-done.8, f32[8,16,16,64]{3,2,1,0:T(8,128)S(1)} %reshape.363, f32[16,64]{1,0:T(8,128)S(1)} %mul.143, ...), kind=kOutput, calls=%fused_computation.26 | convolution fusion | flops 5762048 | bytes 1699840 | tf_op jit(solution)/shard_map/bhij,bihd->bjhd/dot_general | solution.py:69
  95.1 4.6 %multiply_reduce_fusion.1 = (f32[16,64]{1,0:T(8,128)}, f32[8,16,16]{1,2,0:T(8,128)}, f32[8,16,16]{1,2,0:T(8,128)}, f32[8,16,16,64]{3,1,2,0:T(8,128)}) fusion(f32[8,16,16]{1,2,0:T(8,128)S(1)} %copy-done.16, f32[8,16,16]{1,2,0:T(8,128)S(1)} %copy-done.10, f32[8,16,16,64]{3,2,1,0:T(8,128)S(1)} %reshape.361, f32[16,64]{1,0:T(8,128)S(1)} %mul.147, ...), kind=kOutput, calls=%fused_computation.27 | convolution fusion | flops 5762048 | bytes 1699840 | tf_op jit(solution)/shard_map/bhij,bjhd->bihd/dot_general | solution.py:68
  99.8 1.4 stack_reshape.7
  101.1 1.5 copy.122
  102.6 1.5 broadcast_multiply_fusion
  104.1 1.5 copy.123
  105.6 1.6 copy.120
  107.2 1.5 broadcast_multiply_fusion.1
  108.7 1.6 copy.121
  110.2 1.4 stack_reshape.6
  111.6 1.5 copy.117
  113.1 1.5 broadcast_multiply_fusion.2
  114.6 1.5 copy.118
  116.1 1.5 copy.115
  117.6 1.5 broadcast_multiply_fusion.3
  119.1 1.5 copy.116
  120.6 1.3 pad_maximum_fusion
  121.9 1.7 copy.130
  123.7 3.1 %multiply_convert_fusion = bf16[8,16,16,64]{3,1,2,0:T(8,128)(2,1)} fusion(f32[8,16,16,64]{3,1,2,0:T(8,128)} %get-tuple-element.27, f32[8,16,16]{1,2,0:T(8,128)} %copy.123, f32[8,16,16]{1,2,0:T(8,128)} %copy.121, f32[16,64]{1,0:T(8,128)S(1)} %mul.143, f32[8,16,16]{1,2,0:T(8,128)} %copy.106, f32[8,16,16]{1,2,0:T(8,128)} %copy-done.7, ...), kind=kLoop, calls=%fused_computation.28 | loop fusion | flops 1048576 | bytes 1347584 | tf_op jit(solution)/shard_map/convert_element_type | solution.py:75
  126.9 2.0 %multiply_convert_fusion.1 = bf16[8,16,16,64]{3,1,2,0:T(8,128)(2,1)} fusion(f32[8,16,16,64]{3,1,2,0:T(8,128)S(1)} %copy-done.6, f32[8,16,16]{1,2,0:T(8,128)S(1)} %copy-done.18, f32[8,16,16]{1,2,0:T(8,128)S(1)} %copy-done.19, f32[16,64]{1,0:T(8,128)S(1)} %mul.147, f32[8,16,16]{1,2,0:T(8,128)S(1)} %copy-done.17, f32[8,16,16]{1,2,0:T(8,128)S(1)} %copy-done.11, ...), kind=kLoop, calls=%fused_computation.30 | loop fusion | flops 1048576 | bytes 1347584 | tf_op jit(solution)/shard_map/convert_element_type | solution.py:74
  129.5 1.1 reshape_reshape.3
  130.7 1.1 convert_element_type.88
  131.9 1.1 convert_element_type.86
  132.9 24.1 %reduce-scatter.4.cloned.1.call-done = f32[128,2]{1,0:T(8,128)} async-done(((f32[1024,2]{1,0:T(8,128)}), f32[128,2]{1,0:T(8,128)}) %reduce-scatter.4.cloned.1.call-update) | async-done | bytes 1040
  157.1 0.9 copy.131
  158.0 11.7 %psum.8 = f32[2,128]{1,0:T(2,128)S(1)} all-reduce(f32[2,128]{1,0:T(2,128)S(1)} %copy.131), channel_id=1, replica_groups=mesh['enc'=4,'grp'=8] {'enc'}, use_global_device_ids=true, to_apply=%region_19.22 | all-reduce | flops 256 | bytes 2048 | tf_op jit(solution)/shard_map/psum | solution.py:153
  (115 shorter events, 13.2 us)
Async XLA Ops:
  7.2 9.9 %copy-start = (bf16[192,1024]{1,0:T(8,128)(2,1)S(1)}, bf16[192,1024]{1,0:T(8,128)(2,1)}, u32[]{:S(2)}) copy-start(bf16[192,1024]{1,0:T(8,128)(2,1)} %param.13) | copy-start | bytes 1179652
  7.2 0.7 copy-start.21
  8.3 0.7 copy-start.22
  10.8 11.8 %all-to-all-start.2 = ((bf16[4,1,48]{2,1,0:T(2,128)(2,1)}), bf16[4,1,48]{2,1,0:T(2,128)(2,1)S(1)}, u32[]{:S(2)}, u32[]{:S(2)}) async-start(bf16[4,1,48]{2,1,0:T(2,128)(2,1)} %copy.107), calls=%async_computation.2 | async-start | bytes 4096 | tf_op jit(solution)/shard_map/all_to_all | solution.py:145
  17.1 1.0 copy-start.12
  18.1 1.0 copy-start.13
  19.1 1.0 copy-start.14
  37.8 14.0 %all-to-all-start.3 = ((bf16[4,48,1024]{2,1,0:T(8,128)(2,1)}), bf16[4,48,1024]{2,1,0:T(8,128)(2,1)S(1)}, u32[]{:S(2)}, u32[]{:S(2)}) async-start(bf16[4,48,1024]{2,1,0:T(8,128)(2,1)} %bitcast.13), calls=%async_computation.3 | async-start | bytes 786432 | tf_op jit(solution)/shard_map/all_to_all | solution.py:144
  51.8 3.6 %copy-start.20 = (f32[2,1024]{1,0:T(2,128)S(1)}, f32[2,1024]{1,0:T(2,128)}, u32[]{:S(2)}) copy-start(f32[2,1024]{1,0:T(2,128)} %param.17) | copy-start | bytes 24580
  51.8 13.4 %all-to-all-start.4 = ((bf16[4,48,1024]{2,1,0:T(8,128)(2,1)}), bf16[4,48,1024]{2,1,0:T(8,128)(2,1)S(1)}, u32[]{:S(2)}, u32[]{:S(2)}) async-start(bf16[4,48,1024]{2,1,0:T(8,128)(2,1)} %bitcast.16), calls=%async_computation.4 | async-start | bytes 786432 | tf_op jit(solution)/shard_map/all_to_all | solution.py:143
  65.2 13.2 %all-to-all-start = ((bf16[4,48,1024]{2,1,0:T(8,128)(2,1)}), bf16[4,48,1024]{2,1,0:T(8,128)(2,1)S(1)}, u32[]{:S(2)}, u32[]{:S(2)}) async-start(bf16[4,48,1024]{2,1,0:T(8,128)(2,1)} %bitcast.3), calls=%async_computation | async-start | bytes 786432 | tf_op jit(solution)/shard_map/all_to_all | solution.py:141
  68.7 88.4 %reduce-scatter.4.cloned.1.call-start = ((), (), s32[]{:S(2)}) async-start(), calls=%async_computation.6 | async-start | bytes 589824
  82.2 0.8 copy-start.7
  84.5 0.8 copy-start.9
  88.3 1.9 %copy-start.1 = (bf16[8,16,16,64]{3,2,1,0:T(8,128)(2,1)S(1)}, bf16[8,16,16,64]{3,2,1,0:T(8,128)(2,1)}, u32[]{:S(2)}) copy-start(bf16[8,16,16,64]{3,2,1,0:T(8,128)(2,1)} %reshape.354) | copy-start | bytes 786436
  88.3 1.9 %copy-start.3 = (bf16[8,16,16,64]{3,2,1,0:T(8,128)(2,1)S(1)}, bf16[8,16,16,64]{3,2,1,0:T(8,128)(2,1)}, u32[]{:S(2)}) copy-start(bf16[8,16,16,64]{3,2,1,0:T(8,128)(2,1)} %reshape.358) | copy-start | bytes 786436
  90.2 0.8 copy-start.8
  90.2 0.9 copy-start.10
  90.2 0.9 copy-start.15
  90.2 0.9 copy-start.16
  123.7 3.2 %copy-start.6 = (f32[8,16,16,64]{3,1,2,0:T(8,128)S(1)}, f32[8,16,16,64]{3,1,2,0:T(8,128)}, u32[]{:S(2)}) copy-start(f32[8,16,16,64]{3,1,2,0:T(8,128)} %get-tuple-element.26) | copy-start | bytes 1572868
  123.7 3.2 %copy-start.11 = (f32[8,16,16]{1,2,0:T(8,128)S(1)}, f32[8,16,16]{1,2,0:T(8,128)}, u32[]{:S(2)}) copy-start(f32[8,16,16]{1,2,0:T(8,128)} %copy-done.9) | copy-start | bytes 24580
  123.7 3.2 %copy-start.17 = (f32[8,16,16]{1,2,0:T(8,128)S(1)}, f32[8,16,16]{1,2,0:T(8,128)}, u32[]{:S(2)}) copy-start(f32[8,16,16]{1,2,0:T(8,128)} %copy.102) | copy-start | bytes 24580
  123.7 3.2 %copy-start.18 = (f32[8,16,16]{1,2,0:T(8,128)S(1)}, f32[8,16,16]{1,2,0:T(8,128)}, u32[]{:S(2)}) copy-start(f32[8,16,16]{1,2,0:T(8,128)} %copy.118) | copy-start | bytes 24580
  123.7 3.2 %copy-start.19 = (f32[8,16,16]{1,2,0:T(8,128)S(1)}, f32[8,16,16]{1,2,0:T(8,128)}, u32[]{:S(2)}) copy-start(f32[8,16,16]{1,2,0:T(8,128)} %copy.116) | copy-start | bytes 24580
  126.9 2.0 %copy-start.2 = (bf16[8,16,16,64]{3,2,1,0:T(8,128)(2,1)S(1)}, bf16[8,16,16,64]{3,2,1,0:T(8,128)(2,1)}, u32[]{:S(2)}) copy-start(bf16[8,16,16,64]{3,2,1,0:T(8,128)(2,1)} %reshape.354) | copy-start | bytes 786436
  129.5 1.1 copy-start.4
  130.7 1.1 copy-start.5
Sparse Core Ops, SparseCore 0:
  123.8 33.2 reduce-scatter.3
where the time goes:
time: 179 us; the launch traced here: 177 us
  waiting for transfers between devices  50.8 us (28%)
  local copies, waits for them, and re-layouts  36.2 us (20%)
  blocking collectives  27 us (15%)
  other arithmetic  18.2 us (10%)
  starting transfers between devices  16.9 us (9%)
  between operations  14.5 us (8%)
  matrix products  13.5 us (8%)
    unnamed x2, waiting for transfers between devices  24.1 us
    all_to_all x1, blocking collectives, local(): lax.all_to_all(packed[1], 'enc', split_axis=0, concat_axis=0, tiled=True)  15.3 us
    psum x1, blocking collectives, local(): group_total = lax.psum(gain_terms, 'enc')  11.7 us
    all_to_all x1, waiting for transfers between devices, local(): lax.all_to_all(packed[3], 'enc', split_axis=0, concat_axis=0, tiled=True)  9.81 us
    all_to_all x1, waiting for transfers between devices, local(): lax.all_to_all(packed[2], 'enc', split_axis=0, concat_axis=0, tiled=True)  9.75 us
    all_to_all x1, waiting for transfers between devices, local(): lax.all_to_all(packed[0], 'enc', split_axis=0, concat_axis=0, tiled=True)  6.38 us
    all_to_all x1, starting transfers between devices, local(): lax.all_to_all(image_slots, 'enc', split_axis=0, concat_axis=0, tiled=True)  6.32 us
    unnamed x48, local copies, waits for them, and re-layouts  5.74 us
  transfers between devices with their start and end apart: 5, of which 5 were waited for; matrix products, arithmetic and copies ran while one was open for 9% of the time, Pallas kernels for 0%

commit v1 on v0

v1 whole, which is shorter than its diff:
```python
import functools
import math

import jax
import jax.numpy as jnp
from jax import lax
from jax.experimental import pallas as pl
from jax.experimental.pallas import tpu as pltpu
from jax.sharding import PartitionSpec as P

HD = 64
PIECE = 16
P_OWN = 8
LANES = 128
UNIT = 4
EPS = 1e-05
FACTOR = HD ** (-0.5)
MESH = pl.DeviceIdType.MESH
BF = jnp.bfloat16
F32 = jnp.float32


def dot(a, b, da=1, db=0):
    return lax.dot_general(a, b, (((da,), (db,)), ((), ())), preferred_element_type=F32)


def xor(index, flip):
    out, bit = 0, 1
    while bit <= flip or bit == 1:
        have = lax.rem(index // bit, 2)
        out = out + bit * ((1 - have) if flip & bit else have)
        bit *= 2
    return out + (index // bit) * bit


def partners(me, count):
    if count & (count - 1) == 0:
        flips = list(range(count // 2, count)) + list(range(count // 2 - 1, 0, -1))
        return [(xor(me, f), xor(me, f)) for f in flips] + [(me, me)]
    offs = list(range(count // 2, count)) + list(range(count // 2 - 1, 0, -1))
    return [
        (lax.rem(me + o, count), lax.rem(me + count - o, count)) for o in offs
    ] + [(me, me)]


def kernel(
    n, groups, pmax, q_hbm, k_hbm, v_hbm, d_hbm, ids_ref, plan_ref, gains_ref,
    oq_ref, ok_ref, ov_ref, og_ref,
    q_ref, k_ref, v_ref, d_ref, send, recv, acc, gpart, grecv, erecv,
    in_sem, own_sem, send_sem, recv_sem, gs_sem, gr_sem, es_sem, er_sem,
):
    feat = q_ref.shape[1]
    per = pmax // n
    me = lax.axis_index("enc")
    grp = lax.axis_index("grp")
    width = og_ref.shape[1]

    loads = [
        pltpu.make_async_copy(src, dst, in_sem.at[i])
        for i, (src, dst) in enumerate(
            ((q_hbm, q_ref), (k_hbm, k_ref), (v_hbm, v_ref), (d_hbm, d_ref))
        )
    ]
    for load in loads:
        load.start()
    barrier = pltpu.get_barrier_semaphore()
    for off in range(1, n):
        pl.semaphore_signal(
            barrier, inc=1, device_id={"enc": lax.rem(me + off, n)}, device_id_type=MESH
        )
    for off in range(1, groups):
        pl.semaphore_signal(
            barrier, inc=1, device_id={"grp": lax.rem(grp + off, groups)}, device_id_type=MESH
        )

    steps = partners(me, n)
    plan = [plan_ref[0, me, j] for j in range(pmax)]
    slots = []
    for to, _ in steps:
        count = 0
        source = [0] * per
        for j in range(pmax):
            hit = plan[j] == to
            for r in range(per):
                source[r] = jnp.where(jnp.logical_and(hit, count == r), j, source[r])
            count = count + hit.astype(jnp.int32)
        slots += [(source[r], jnp.where(count > r, 1, 0)) for r in range(per)]

    rows = UNIT * PIECE
    row = lax.broadcasted_iota(jnp.int32, (rows, LANES), 0)
    lane = lax.broadcasted_iota(jnp.int32, (rows, LANES), 1)
    first = lane < HD
    m0 = first.astype(F32).astype(BF)
    m1 = (1.0 - first.astype(F32)).astype(BF)
    brow = lax.broadcasted_iota(jnp.int32, (LANES, LANES), 0)
    bcol = lax.broadcasted_iota(jnp.int32, (LANES, LANES), 1)
    blk = ((brow // HD) == (bcol // HD)).astype(F32).astype(BF)
    blk2 = jnp.concatenate([blk, blk], 0)

    def seg(x):
        high = x.astype(BF)
        low = (x - high.astype(F32)).astype(BF)
        return dot(jnp.concatenate([high, low], 1), blk2)

    def both(x):
        return jnp.concatenate([x * m0, x * m1], 0)

    def halves(x):
        return jnp.where(first, x[:rows], x[rows:])

    acc[...] = jnp.zeros_like(acc)
    gpart[...] = jnp.zeros_like(gpart)
    for load in loads:
        load.wait()

    def pick(values):
        out = values[-1]
        for i in range(UNIT - 2, -1, -1):
            out = jnp.where(row < (i + 1) * PIECE, values[i], out)
        return out

    def unit(chunk):
        source = [s for s, _ in slots[chunk * UNIT : (chunk + 1) * UNIT]]
        live = pick([f for _, f in slots[chunk * UNIT : (chunk + 1) * UNIT]]) > 0
        starts = [s * PIECE for s in source]
        ids = ids_ref[...]
        wide = ids.shape[1]
        wrow = lax.broadcasted_iota(jnp.int32, (rows, wide), 0)
        wlane = lax.broadcasted_iota(jnp.int32, (rows, wide), 1)
        base = starts[-1]
        for i in range(UNIT - 2, -1, -1):
            base = jnp.where(wrow < (i + 1) * PIECE, starts[i], base)
        chosen = wlane == base + lax.rem(wrow, PIECE)
        number = jnp.sum(jnp.where(chosen, ids, 0).astype(F32), axis=1, keepdims=True)
        chosen = chosen.astype(F32).astype(BF)
        place = (lane - (row // PIECE) * PIECE).astype(F32)
        hot = (place == number).astype(F32).astype(BF)
        same = dot(hot, jnp.concatenate([hot, hot], 0), 1, 1) > 0.5

        def some(half, carry):
            lanes = [
                pl.ds(pl.multiple_of((half * PAIRS + i) * LANES, LANES), LANES)
                for i in range(PAIRS)
            ]

            def take(ref):
                return [dot(chosen, ref[:, ln]).astype(BF) for ln in lanes]

            def normed(xs, g):
                mean = [dot(x, blk) * (1 / HD) for x in xs]
                cen = [x.astype(F32) - m for x, m in zip(xs, mean)]
                var = [seg(c * c) * (1 / HD) for c in cen]
                inv = [lax.rsqrt(v + EPS) for v in var]
                nor = [c * i for c, i in zip(cen, inv)]
                hat = [(x * gg).astype(BF) for x, gg in zip(nor, g)]
                return nor, inv, hat

            gq = [gains_ref[0:1, ln] for ln in lanes]
            gk = [gains_ref[1:2, ln] for ln in lanes]
            nq, iq, hq = normed(take(q_ref), gq)
            nk, ik, hk = normed(take(k_ref), gk)
            cot = [jnp.where(live, x.astype(F32), 0.0).astype(BF) for x in take(d_ref)]
            hk2 = [both(x) for x in hk]
            v2 = [both(x) for x in take(v_ref)]
            score = [dot(a, b, 1, 1) * FACTOR for a, b in zip(hq, hk2)]
            dprob = [dot(a, b, 1, 1) for a, b in zip(cot, v2)]
            weight = [jnp.where(same, jnp.exp(s), 0.0) for s in score]
            total = [seg(w) for w in weight]
            prob = [w / t for w, t in zip(weight, total)]
            probb = [p.astype(BF) for p in prob]
            delta = [seg(p.astype(F32) * x) for p, x in zip(probb, dprob)]
            dscore = [
                (p * (x - y) * FACTOR).astype(BF) for p, x, y in zip(prob, dprob, delta)
            ]
            dval = [halves(dot(p, c, 0, 0)) for p, c in zip(probb, cot)]
            dq = [dot(a, b) for a, b in zip(dscore, hk2)]
            dk = [halves(dot(a, b, 0, 0)) for a, b in zip(dscore, hq)]

            def back(dh, nor, inv, g, where):
                dn = [a * gg for a, gg in zip(dh, g)]
                one = [seg(a) * (1 / HD) for a in dn]
                two = [seg(a * b) * (1 / HD) for a, b in zip(dn, nor)]
                for i, ln in enumerate(lanes):
                    acc[where : where + 8, ln] += jnp.sum(
                        (dh[i] * nor[i]).reshape(rows // 8, 8, LANES), 0
                    )
                return [
                    i * (a - b - c * d) for i, a, b, c, d in zip(inv, dn, one, nor, two)
                ]

            rq = back(dq, nq, iq, gq, 0)
            rk = back(dk, nk, ik, gk, 8)
            for a, result in enumerate((rq, rk, dval)):
                for i in range(PAIRS):
                    at_lane = pl.multiple_of(a * feat + (half * PAIRS + i) * LANES, LANES)
                    send[chunk * rows : (chunk + 1) * rows, pl.ds(at_lane, LANES)] = result[
                        i
                    ].astype(BF)
            return carry

        lax.fori_loop(0, feat // LANES // PAIRS, some, 0)

    copies = []
    for chunk in range(pmax // UNIT):
        unit(chunk)
        if chunk == 0:
            pl.semaphore_wait(barrier, n - 1 + groups - 1)
        low, high = chunk * UNIT, (chunk + 1) * UNIT
        for step in range(n - 1):
            a, b = max(low, step * per), min(high, (step + 1) * per)
            if a >= b:
                continue
            to, frm = steps[step]
            count = (b - a) * PIECE
            shift = (a - step * per) * PIECE
            sem = len(copies)

            def copy(owner_row):
                return pltpu.make_async_remote_copy(
                    src_ref=send.at[pl.ds(a * PIECE, count)],
                    dst_ref=recv.at[
                        pl.ds(pl.multiple_of(owner_row * (per * PIECE) + shift, PIECE), count)
                    ],
                    send_sem=send_sem.at[sem],
                    recv_sem=recv_sem.at[sem],
                    device_id={"enc": to},
                    device_id_type=MESH,
                )

            copy(me).start()
            copies.append((copy(me), copy(frm)))
    own = pltpu.make_async_copy(
        send.at[pl.ds((n - 1) * per * PIECE, per * PIECE)],
        recv.at[pl.ds(pl.multiple_of(me * (per * PIECE), PIECE), per * PIECE)],
        own_sem,
    )
    own.start()

    gq = jnp.sum(acc[0:8, :], 0, keepdims=True)
    gk = jnp.sum(acc[8:16, :], 0, keepdims=True)
    for j in range(groups):
        gpart[j, 0:1, 0:width] = gq[:, j * width : (j + 1) * width]
        gpart[j, 1:2, 0:width] = gk[:, j * width : (j + 1) * width]
    shares = []
    for off in range(1, groups):
        to = lax.rem(grp + off, groups)
        share = pltpu.make_async_remote_copy(
            src_ref=gpart.at[to],
            dst_ref=grecv.at[off],
            send_sem=gs_sem.at[off],
            recv_sem=gr_sem.at[off],
            device_id={"grp": to},
            device_id_type=MESH,
        )
        share.start()
        shares.append(share)
    part = gpart[grp]
    for off, share in enumerate(shares, 1):
        share.wait_recv()
        part = part + grecv[off]
    erecv[me] = part
    sums = []
    for i, (to, frm) in enumerate(steps[:-1]):
        both_ways = [
            pltpu.make_async_remote_copy(
                src_ref=erecv.at[me],
                dst_ref=erecv.at[at],
                send_sem=es_sem.at[i],
                recv_sem=er_sem.at[i],
                device_id={"enc": to},
                device_id_type=MESH,
            )
            for at in (me, frm)
        ]
        both_ways[0].start()
        sums.append(both_ways)
    index = [0] * P_OWN
    start = 0
    for s in range(n):
        got = 0
        for j in range(pmax):
            got = got + (plan_ref[0, s, j] == me).astype(jnp.int32)
        for p in range(P_OWN):
            inside = jnp.logical_and(p >= start, p < start + got)
            index[p] = jnp.where(inside, s * per + p - start, index[p])
        start = start + got
    for out, arrived in sums:
        arrived.wait_recv()
    total = erecv[0]
    for s in range(1, n):
        total = total + erecv[s]
    og_ref[...] = total[0:2, 0:width] / math.sqrt(n * groups * P_OWN * PIECE)

    own.wait()
    for out, arrived in copies:
        arrived.wait_recv()
    orow = lax.broadcasted_iota(jnp.int32, (P_OWN * PIECE, pmax * PIECE), 0)
    olane = lax.broadcasted_iota(jnp.int32, (P_OWN * PIECE, pmax * PIECE), 1)
    base = index[-1] * PIECE
    for p in range(P_OWN - 2, -1, -1):
        base = jnp.where(orow < (p + 1) * PIECE, index[p] * PIECE, base)
    order = (olane == base + lax.rem(orow, PIECE)).astype(F32).astype(BF)
    for a, out in enumerate((oq_ref, ok_ref, ov_ref)):
        for low in range(0, feat, feat // 2):
            high = low + feat // 2
            out[:, low:high] = dot(order, recv[:, a * feat + low : a * feat + high]).astype(BF)
    for out, _ in copies:
        out.wait_send()
    for share in shares:
        share.wait_send()
    for out, _ in sums:
        out.wait_send()


PAIRS = 4


def local(query_raw, key_raw, value_rows, out_cotangent, image_ids, owners, gains):
    n = lax.axis_size("enc")
    groups = lax.axis_size("grp")
    pmax = owners.shape[-1]
    rows, feat = query_raw.shape
    own_rows = P_OWN * PIECE
    vmem = pl.BlockSpec(memory_space=pltpu.VMEM)
    hbm = pl.BlockSpec(memory_space=pl.ANY)
    grad = jax.ShapeDtypeStruct((own_rows, feat), BF)
    dma = pltpu.SemaphoreType.DMA
    many = n + pmax // UNIT
    return pl.pallas_call(
        functools.partial(kernel, n, groups, pmax),
        out_shape=(grad, grad, grad, jax.ShapeDtypeStruct((2, feat // groups), F32)),
        in_specs=[hbm] * 4
        + [vmem, pl.BlockSpec(memory_space=pltpu.SMEM), vmem],
        out_specs=(vmem,) * 4,
        scratch_shapes=[pltpu.VMEM((rows, feat), BF)] * 4
        + [
            pltpu.VMEM((rows, 3 * feat), BF),
            pltpu.VMEM((rows, 3 * feat), BF),
            pltpu.VMEM((16, feat), F32),
            pltpu.VMEM((groups, 8, LANES), F32),
            pltpu.VMEM((groups, 8, LANES), F32),
            pltpu.VMEM((n, 8, LANES), F32),
            dma((4,)),
            dma,
            dma((many,)),
            dma((many,)),
            dma((groups,)),
            dma((groups,)),
            dma((n,)),
            dma((n,)),
        ],
        compiler_params=pltpu.CompilerParams(
            collective_id=0, has_side_effects=True, vmem_limit_bytes=32 * 1024 * 1024
        ),
        cost_estimate=pl.CostEstimate(
            flops=2 * 24 * rows * feat * LANES, bytes_accessed=14 * rows * feat, transcendentals=rows * feat
        ),
    )(query_raw, key_raw, value_rows, out_cotangent, image_ids.reshape(1, rows), owners, gains)


def solution(mesh):
    rows = P(("enc", "grp"), None)
    return jax.shard_map(
        local,
        mesh=mesh,
        in_specs=(rows, rows, rows, rows, P(("enc", "grp")), P("grp", None, None), P()),
        out_specs=(rows, rows, rows, P(None, "grp")),
        check_vma=False,
    )
```

time: 179 us -> 46.1 us (0.26)
  waiting for transfers between devices: 50.8 us -> 0 us
  Pallas kernels: 0 us -> 36.4 us
  local copies, waits for them, and re-layouts: 36.2 us -> 8.7 us
  blocking collectives: 27 us -> 0 us
  other arithmetic: 18.2 us -> 0 us
  starting transfers between devices: 16.9 us -> 0 us
  between operations: 14.5 us -> 0.66 us
  matrix products: 13.5 us -> 0 us
    pallas_call x0 -> x1, Pallas kernels: none -> 36.4 us  [local(): pl.pallas_call(functools.partial(kernel, n, groups, pmax), out_shape=(gra...]
    all_to_all x4 -> x0, waiting for transfers between devices: 26.6 us -> none  [the longest x1 9.81 us: local(): lax.all_to_all(packed[3], 'enc', split_axis=0, concat_axis=0, tiled=True)]
    unnamed x2 -> x0, waiting for transfers between devices: 24.1 us -> none
    all_to_all x4 -> x0, starting transfers between devices: 16.8 us -> none  [the longest x1 6.32 us: local(): lax.all_to_all(image_slots, 'enc', split_axis=0, concat_axis=0, tiled=True)]
    all_to_all x1 -> x0, blocking collectives: 15.3 us -> none  [local(): lax.all_to_all(packed[1], 'enc', split_axis=0, concat_axis=0, tiled=True)]
    psum x1 -> x0, blocking collectives: 11.7 us -> none  [local(): group_total = lax.psum(gain_terms, 'enc')]
    dot_general x5 -> x0, matrix products: 11.3 us -> none  [the longest x1 4.63 us: piece_grads(): jnp.einsum('bhij,bjhd->bihd', d_score, k_hat, preferred_element_type=jnp....]
    div x7 -> x0, other arithmetic: 6.43 us -> none  [the longest x2 2.94 us: norm_back(): jnp.mean(d_norm, -1, keepdims=True)]
  transfers between devices with their start and end apart: 5 -> 0, of which waited for: 5 -> 0; matrix products, arithmetic and copies ran while one was open for 9% -> 0% of each run, Pallas kernels for 0% -> 0%
where the time goes in v1:
time: 46.1 us; the launch traced here: 45.7 us
  Pallas kernels  36.4 us (79%)
  local copies, waits for them, and re-layouts  8.7 us (19%)
  between operations  0.66 us (1%)
    pallas_call x1, Pallas kernels, local(): pl.pallas_call(functools.partial(kernel, n, groups, pmax), out_shape=(gra...  36.4 us
    unnamed x18, local copies, waits for them, and re-layouts  8.7 us

profile of v1, /device:TPU:0, one launch (start us, length us, event | category | flops | bytes accessed | tf_op | source)
XLA Modules:
  0.0 45.7 jit_solution(1622747763038227440)
XLA Ops:
  0.6 0.0 copy-start.6
  0.6 0.7 %copy-done.6 = s32[192]{0:T(256)S(1)} copy-done((s32[192]{0:T(256)S(1)}, s32[192]{0:T(256)}, u32[]{:S(2)}) %copy-start.6) | copy-done | bytes 792
  1.3 0.0 copy-start
  1.3 1.0 %copy-done = bf16[192,1024]{1,0:T(8,128)(2,1)S(1)} copy-done((bf16[192,1024]{1,0:T(8,128)(2,1)S(1)}, bf16[192,1024]{1,0:T(8,128)(2,1)}, u32[]{:S(2)}) %copy-start) | copy-done | bytes 393240
  2.3 0.0 copy-start.1
  2.3 1.0 %copy-done.1 = bf16[192,1024]{1,0:T(8,128)(2,1)S(1)} copy-done((bf16[192,1024]{1,0:T(8,128)(2,1)S(1)}, bf16[192,1024]{1,0:T(8,128)(2,1)}, u32[]{:S(2)}) %copy-start.1) | copy-done | bytes 393240
  3.3 0.0 copy-start.2
  3.3 1.0 %copy-done.2 = bf16[192,1024]{1,0:T(8,128)(2,1)S(1)} copy-done((bf16[192,1024]{1,0:T(8,128)(2,1)S(1)}, bf16[192,1024]{1,0:T(8,128)(2,1)}, u32[]{:S(2)}) %copy-start.2) | copy-done | bytes 393240
  4.3 0.0 copy-start.3
  4.3 1.0 %copy-done.3 = bf16[192,1024]{1,0:T(8,128)(2,1)S(1)} copy-done((bf16[192,1024]{1,0:T(8,128)(2,1)S(1)}, bf16[192,1024]{1,0:T(8,128)(2,1)}, u32[]{:S(2)}) %copy-start.3) | copy-done | bytes 393240
  5.3 0.0 copy-start.4
  5.3 0.7 %copy-done.4 = f32[2,1024]{1,0:T(2,128)S(1)} copy-done((f32[2,1024]{1,0:T(2,128)S(1)}, f32[2,1024]{1,0:T(2,128)}, u32[]{:S(2)}) %copy-start.4) | copy-done | bytes 8216
  6.0 0.0 copy-start.5
  6.0 0.7 %copy-done.5 = s32[1,4,12]{2,1,0:T(4,128)S(1)} copy-done((s32[1,4,12]{2,1,0:T(4,128)S(1)}, s32[1,4,12]{2,1,0:T(4,128)}, u32[]{:S(2)}) %copy-start.5) | copy-done | bytes 216
  6.7 36.4 %shard_map.102 = (bf16[128,1024]{1,0:T(8,128)(2,1)S(1)}, bf16[128,1024]{1,0:T(8,128)(2,1)S(1)}, bf16[128,1024]{1,0:T(8,128)(2,1)S(1)}, f32[2,128]{1,0:T(2,128)S(1)}) custom-call(bf16[192,1024]{1,0:T(8,128)(2,1)S(1)} %copy-done, bf16[192,1024]{1,0:T(8,128)(2,1)S(1)} %copy-done.1, bf16[192,1024]{1,0:T(8,128)(2,1)S(1)} %copy-done.2, ...), custom_call_target="tpu_custom_call" | custom-call | flops 1207959552 | bytes 2752512 | tf_op jit(solution)/shard_map/pallas_call | solution.py:329
  43.0 0.7 %copy.15 = bf16[128,1024]{1,0:T(8,128)(2,1)} copy(bf16[128,1024]{1,0:T(8,128)(2,1)S(1)} %get-tuple-element.8) | data formatting | bytes 524288
  43.7 0.7 %copy.16 = bf16[128,1024]{1,0:T(8,128)(2,1)} copy(bf16[128,1024]{1,0:T(8,128)(2,1)S(1)} %get-tuple-element.9) | data formatting | bytes 524288
  44.5 0.7 %copy.17 = bf16[128,1024]{1,0:T(8,128)(2,1)} copy(bf16[128,1024]{1,0:T(8,128)(2,1)S(1)} %get-tuple-element.10) | data formatting | bytes 524288
  45.2 0.6 %copy.18 = f32[2,128]{1,0:T(2,128)} copy(f32[2,128]{1,0:T(2,128)S(1)} %get-tuple-element.11) | data formatting | bytes 2048
Async XLA Ops:
  0.6 0.7 %copy-start.6 = (s32[192]{0:T(256)S(1)}, s32[192]{0:T(256)}, u32[]{:S(2)}) copy-start(s32[192]{0:T(256)} %param.11) | copy-start | bytes 2308
  1.3 1.0 %copy-start = (bf16[192,1024]{1,0:T(8,128)(2,1)S(1)}, bf16[192,1024]{1,0:T(8,128)(2,1)}, u32[]{:S(2)}) copy-start(bf16[192,1024]{1,0:T(8,128)(2,1)} %q_hbm.1) | copy-start | bytes 1179652
  2.3 1.0 %copy-start.1 = (bf16[192,1024]{1,0:T(8,128)(2,1)S(1)}, bf16[192,1024]{1,0:T(8,128)(2,1)}, u32[]{:S(2)}) copy-start(bf16[192,1024]{1,0:T(8,128)(2,1)} %k_hbm.1) | copy-start | bytes 1179652
  3.3 1.0 %copy-start.2 = (bf16[192,1024]{1,0:T(8,128)(2,1)S(1)}, bf16[192,1024]{1,0:T(8,128)(2,1)}, u32[]{:S(2)}) copy-start(bf16[192,1024]{1,0:T(8,128)(2,1)} %v_hbm.1) | copy-start | bytes 1179652
  4.3 1.0 %copy-start.3 = (bf16[192,1024]{1,0:T(8,128)(2,1)S(1)}, bf16[192,1024]{1,0:T(8,128)(2,1)}, u32[]{:S(2)}) copy-start(bf16[192,1024]{1,0:T(8,128)(2,1)} %d_hbm.1) | copy-start | bytes 1179652
  5.3 0.7 %copy-start.4 = (f32[2,1024]{1,0:T(2,128)S(1)}, f32[2,1024]{1,0:T(2,128)}, u32[]{:S(2)}) copy-start(f32[2,1024]{1,0:T(2,128)} %gains_ref.1) | copy-start | bytes 24580
  6.0 0.7 %copy-start.5 = (s32[1,4,12]{2,1,0:T(4,128)S(1)}, s32[1,4,12]{2,1,0:T(4,128)}, u32[]{:S(2)}) copy-start(s32[1,4,12]{2,1,0:T(4,128)} %plan_ref.1) | copy-start | bytes 580

commit v2 on v1

--- a/solution.py
+++ b/solution.py
@@ -44,10 +44,11 @@
 
 
 def kernel(
-    n, groups, pmax, q_hbm, k_hbm, v_hbm, d_hbm, ids_ref, plan_ref, gains_ref,
-    oq_ref, ok_ref, ov_ref, og_ref,
-    q_ref, k_ref, v_ref, d_ref, send, recv, acc, gpart, grecv, erecv,
-    in_sem, own_sem, send_sem, recv_sem, gs_sem, gr_sem, es_sem, er_sem,
+    n, groups, pmax, q_hbm, k_hbm, v_hbm, d_hbm, ids_hbm, plan_hbm, gains_hbm,
+    recv, order_hbm, og_hbm,
+    q_ref, k_ref, v_ref, d_ref, ids_ref, plan_ref, gains_ref,
+    order_ref, og_ref, send, acc, gpart, grecv, erecv,
+    in_sem, out_sem, own_sem, send_sem, recv_sem, gs_sem, gr_sem, es_sem, er_sem,
 ):
     feat = q_ref.shape[1]
     per = pmax // n
@@ -58,7 +59,10 @@
     loads = [
         pltpu.make_async_copy(src, dst, in_sem.at[i])
         for i, (src, dst) in enumerate(
-            ((q_hbm, q_ref), (k_hbm, k_ref), (v_hbm, v_ref), (d_hbm, d_ref))
+            (
+                (plan_hbm, plan_ref), (ids_hbm, ids_ref), (gains_hbm, gains_ref),
+                (q_hbm, q_ref), (k_hbm, k_ref), (v_hbm, v_ref), (d_hbm, d_ref),
+            )
         )
     ]
     for load in loads:
@@ -74,6 +78,7 @@
         )
 
     steps = partners(me, n)
+    loads[0].wait()
     plan = [plan_ref[0, me, j] for j in range(pmax)]
     slots = []
     for to, _ in steps:
@@ -110,7 +115,7 @@
 
     acc[...] = jnp.zeros_like(acc)
     gpart[...] = jnp.zeros_like(gpart)
-    for load in loads:
+    for load in loads[1:]:
         load.wait()
 
     def pick(values):
@@ -119,7 +124,7 @@
             out = jnp.where(row < (i + 1) * PIECE, values[i], out)
         return out
 
-    def unit(chunk):
+    def unit(chunk, leave):
         source = [s for s, _ in slots[chunk * UNIT : (chunk + 1) * UNIT]]
         live = pick([f for _, f in slots[chunk * UNIT : (chunk + 1) * UNIT]]) > 0
         starts = [s * PIECE for s in source]
@@ -192,43 +197,50 @@
             rk = back(dk, nk, ik, gk, 8)
             for a, result in enumerate((rq, rk, dval)):
                 for i in range(PAIRS):
-                    at_lane = pl.multiple_of(a * feat + (half * PAIRS + i) * LANES, LANES)
+                    at_lane = pl.multiple_of(half * (3 * part) + a * part + i * LANES, LANES)
                     send[chunk * rows : (chunk + 1) * rows, pl.ds(at_lane, LANES)] = result[
                         i
                     ].astype(BF)
+            for copy in leave(half):
+                copy.start()
             return carry
 
-        lax.fori_loop(0, feat // LANES // PAIRS, some, 0)
-
-    copies = []
+        lax.fori_loop(0, halves_count, some, 0)
+
+    part = PAIRS * LANES
+    halves_count = feat // part
+    spans = []
     for chunk in range(pmax // UNIT):
-        unit(chunk)
-        if chunk == 0:
-            pl.semaphore_wait(barrier, n - 1 + groups - 1)
         low, high = chunk * UNIT, (chunk + 1) * UNIT
         for step in range(n - 1):
             a, b = max(low, step * per), min(high, (step + 1) * per)
-            if a >= b:
-                continue
-            to, frm = steps[step]
-            count = (b - a) * PIECE
-            shift = (a - step * per) * PIECE
-            sem = len(copies)
-
-            def copy(owner_row):
-                return pltpu.make_async_remote_copy(
-                    src_ref=send.at[pl.ds(a * PIECE, count)],
-                    dst_ref=recv.at[
-                        pl.ds(pl.multiple_of(owner_row * (per * PIECE) + shift, PIECE), count)
-                    ],
-                    send_sem=send_sem.at[sem],
-                    recv_sem=recv_sem.at[sem],
-                    device_id={"enc": to},
-                    device_id_type=MESH,
-                )
-
-            copy(me).start()
-            copies.append((copy(me), copy(frm)))
+            if a < b:
+                spans.append((chunk, step, a, b))
+
+    def span_copy(which, half, arriving):
+        _, step, a, b = spans[which]
+        to, frm = steps[step]
+        count = (b - a) * PIECE
+        shift = (a - step * per) * PIECE
+        at_row = (frm if arriving else me) * (per * PIECE) + shift
+        lanes = pl.ds(pl.multiple_of(half * (3 * part), 3 * part), 3 * part)
+        return pltpu.make_async_remote_copy(
+            src_ref=send.at[pl.ds(a * PIECE, count), lanes],
+            dst_ref=recv.at[pl.ds(pl.multiple_of(at_row, PIECE), count), lanes],
+            send_sem=send_sem.at[which, half],
+            recv_sem=recv_sem.at[which, half],
+            device_id={"enc": to},
+            device_id_type=MESH,
+        )
+
+    pl.semaphore_wait(barrier, n - 1 + groups - 1)
+    for chunk in range(pmax // UNIT):
+        unit(
+            chunk,
+            lambda half: [
+                span_copy(w, half, False) for w in range(len(spans)) if spans[w][0] == chunk
+            ],
+        )
     own = pltpu.make_async_copy(
         send.at[pl.ds((n - 1) * per * PIECE, per * PIECE)],
         recv.at[pl.ds(pl.multiple_of(me * (per * PIECE), PIECE), per * PIECE)],
@@ -254,11 +266,11 @@
         )
         share.start()
         shares.append(share)
-    part = gpart[grp]
+    mine = gpart[grp]
     for off, share in enumerate(shares, 1):
         share.wait_recv()
-        part = part + grecv[off]
-    erecv[me] = part
+        mine = mine + grecv[off]
+    erecv[me] = mine
     sums = []
     for i, (to, frm) in enumerate(steps[:-1]):
         both_ways = [
@@ -291,25 +303,65 @@
         total = total + erecv[s]
     og_ref[...] = total[0:2, 0:width] / math.sqrt(n * groups * P_OWN * PIECE)
 
-    own.wait()
-    for out, arrived in copies:
-        arrived.wait_recv()
     orow = lax.broadcasted_iota(jnp.int32, (P_OWN * PIECE, pmax * PIECE), 0)
     olane = lax.broadcasted_iota(jnp.int32, (P_OWN * PIECE, pmax * PIECE), 1)
     base = index[-1] * PIECE
     for p in range(P_OWN - 2, -1, -1):
         base = jnp.where(orow < (p + 1) * PIECE, index[p] * PIECE, base)
-    order = (olane == base + lax.rem(orow, PIECE)).astype(F32).astype(BF)
-    for a, out in enumerate((oq_ref, ok_ref, ov_ref)):
-        for low in range(0, feat, feat // 2):
-            high = low + feat // 2
-            out[:, low:high] = dot(order, recv[:, a * feat + low : a * feat + high]).astype(BF)
-    for out, _ in copies:
-        out.wait_send()
+    order_ref[...] = (olane == base + lax.rem(orow, PIECE)).astype(F32).astype(BF)
+    small = [
+        pltpu.make_async_copy(order_ref, order_hbm, out_sem.at[0]),
+        pltpu.make_async_copy(og_ref, og_hbm, out_sem.at[1]),
+    ]
+    for copy in small:
+        copy.start()
+    own.wait()
+    for copy in small:
+        copy.wait()
+    for half in range(halves_count):
+        for w in range(len(spans)):
+            span_copy(w, half, True).wait_recv()
+    for half in range(halves_count):
+        for w in range(len(spans)):
+            span_copy(w, half, False).wait_send()
     for share in shares:
         share.wait_send()
     for out, _ in sums:
         out.wait_send()
+
+
+def place(recv_hbm, order_hbm, gain, oq, ok, ov, og, recv, order, buf, in_sem, sem):
+    feat = oq.shape[1]
+    part = PAIRS * LANES
+    count = feat // part
+    first = pltpu.make_async_copy(order_hbm, order, in_sem.at[3 * count])
+    first.start()
+    loads = []
+    for a in range(3):
+        for half in range(count):
+            low = half * (3 * part) + a * part
+            lanes = slice(low, low + part)
+            loads.append(
+                pltpu.make_async_copy(
+                    recv_hbm.at[:, lanes], recv.at[:, lanes], in_sem.at[a * count + half]
+                )
+            )
+            loads[-1].start()
+    copies = [pltpu.make_async_copy(gain, og, sem.at[3])]
+    copies[0].start()
+    first.wait()
+    pick = order[...]
+    for a, out in enumerate((oq, ok, ov)):
+        for half in range(count):
+            loads[a * count + half].wait()
+            low = half * (3 * part) + a * part
+            buf[a, :, half * part : (half + 1) * part] = dot(
+                pick, recv[:, low : low + part]
+            ).astype(BF)
+        copies.append(pltpu.make_async_copy(buf.at[a], out, sem.at[a]))
+        copies[-1].start()
+    for copy in copies:
+        copy.wait()
 
 
 PAIRS = 4
@@ -321,41 +373,66 @@
     pmax = owners.shape[-1]
     rows, feat = query_raw.shape
     own_rows = P_OWN * PIECE
-    vmem = pl.BlockSpec(memory_space=pltpu.VMEM)
-    hbm = pl.BlockSpec(memory_space=pl.ANY)
+    hbm = pl.BlockSpec(memory_space=pltpu.HBM)
     grad = jax.ShapeDtypeStruct((own_rows, feat), BF)
+    gain = jax.ShapeDtypeStruct((2, feat // groups), F32)
     dma = pltpu.SemaphoreType.DMA
     many = n + pmax // UNIT
-    return pl.pallas_call(
+    halves_count = feat // (PAIRS * LANES)
+    arrived, order, share = pl.pallas_call(
         functools.partial(kernel, n, groups, pmax),
-        out_shape=(grad, grad, grad, jax.ShapeDtypeStruct((2, feat // groups), F32)),
-        in_specs=[hbm] * 4
-        + [vmem, pl.BlockSpec(memory_space=pltpu.SMEM), vmem],
-        out_specs=(vmem,) * 4,
+        out_shape=(
+            jax.ShapeDtypeStruct((rows, 3 * feat), BF),
+            jax.ShapeDtypeStruct((own_rows, rows), BF),
+            gain,
+        ),
+        in_specs=[hbm] * 7,
+        out_specs=(hbm,) * 3,
         scratch_shapes=[pltpu.VMEM((rows, feat), BF)] * 4
         + [
-            pltpu.VMEM((rows, 3 * feat), BF),
+            pltpu.VMEM((1, rows), jnp.int32),
+            pltpu.SMEM(owners.shape, jnp.int32),
+            pltpu.VMEM(gains.shape, F32),
+            pltpu.VMEM((own_rows, rows), BF),
+            pltpu.VMEM(gain.shape, F32),
             pltpu.VMEM((rows, 3 * feat), BF),
             pltpu.VMEM((16, feat), F32),
             pltpu.VMEM((groups, 8, LANES), F32),
             pltpu.VMEM((groups, 8, LANES), F32),
             pltpu.VMEM((n, 8, LANES), F32),
-            dma((4,)),
+            dma((7,)),
+            dma((2,)),
             dma,
-            dma((many,)),
-            dma((many,)),
+            dma((many, halves_count)),
+            dma((many, halves_count)),
             dma((groups,)),
             dma((groups,)),
             dma((n,)),
             dma((n,)),
         ],
         compiler_params=pltpu.CompilerParams(
-            collective_id=0, has_side_effects=True, vmem_limit_bytes=32 * 1024 * 1024
+            collective_id=0, has_side_effects=True, vmem_limit_bytes=62 * 1024 * 1024
         ),
         cost_estimate=pl.CostEstimate(
-            flops=2 * 24 * rows * feat * LANES, bytes_accessed=14 * rows * feat, transcendentals=rows * feat
+            flops=2 * 24 * rows * feat * LANES,
+            bytes_accessed=14 * rows * feat,
+            transcendentals=rows * feat,
         ),
     )(query_raw, key_raw, value_rows, out_cotangent, image_ids.reshape(1, rows), owners, gains)
+    return pl.pallas_call(
+        place,
+        out_shape=(grad, grad, grad, gain),
+        in_specs=[hbm] * 3,
+        out_specs=(hbm,) * 4,
+        scratch_shapes=[
+            pltpu.VMEM((rows, 3 * feat), BF),
+            pltpu.VMEM((own_rows, rows), BF),
+            pltpu.VMEM((3, own_rows, feat), BF),
+            dma((3 * halves_count + 1,)),
+            dma((4,)),
+        ],
+        compiler_params=pltpu.CompilerParams(vmem_limit_bytes=62 * 1024 * 1024),
+    )(arrived, order, share)
 
 
 def solution(mesh):

time: 46.1 us -> 40 us (0.87)
  local copies, waits for them, and re-layouts: 8.7 us -> 0 us
  Pallas kernels: 36.4 us -> 39.2 us
    unnamed x18 -> x0, local copies, waits for them, and re-layouts: 8.7 us -> none
    pallas_call x1 -> x2, Pallas kernels: 36.4 us -> 39.2 us  [the longest x1 36.4 us: local(): pl.pallas_call(functools.partial(kernel, n, groups, pmax), out_shape=(jax...]
where the time goes in v2:
time: 40 us; the launch traced here: 39.9 us
  Pallas kernels  39.2 us (98%)
  between operations  0.64 us (2%)
    pallas_call x1, Pallas kernels, local(): pl.pallas_call(functools.partial(kernel, n, groups, pmax), out_shape=(jax...  36.4 us
    pallas_call x1, Pallas kernels, local(): pl.pallas_call(place, out_shape=(grad, grad, grad, gain), in_specs=[hbm]...  2.87 us

profile of v2, /device:TPU:0, one launch (start us, length us, event | category | flops | bytes accessed | tf_op | source)
XLA Modules:
  0.0 39.9 jit_solution(16902932941151676730)
XLA Ops:
  0.6 36.4 %shard_map.102 = (bf16[192,3072]{1,0:T(8,128)(2,1)}, bf16[128,192]{1,0:T(8,128)(2,1)}, f32[2,128]{1,0:T(2,128)}) custom-call(bf16[192,1024]{1,0:T(8,128)(2,1)} %q_hbm.1, bf16[192,1024]{1,0:T(8,128)(2,1)} %k_hbm.1, bf16[192,1024]{1,0:T(8,128)(2,1)} %v_hbm.1, bf16[192,1024]{1,0:T(8,128)(2,1)} %d_hbm.1, s32[1,192]{1,0:T(1,128)} %bitcast.1, ...), custom_call_target="tpu_custom_call" | custom-call | flops 1207959552 | bytes 2752512 | tf_op jit(solution)/shard_map/pallas_call | solution.py:382
  37.0 2.9 %shard_map.103 = (bf16[128,1024]{1,0:T(8,128)(2,1)}, bf16[128,1024]{1,0:T(8,128)(2,1)}, bf16[128,1024]{1,0:T(8,128)(2,1)}, f32[2,128]{1,0:T(2,128)}) custom-call(bf16[192,3072]{1,0:T(8,128)(2,1)} %get-tuple-element.7.recv_hbm, bf16[128,192]{1,0:T(8,128)(2,1)} %get-tuple-element.8.order_hbm, f32[2,128]{1,0:T(2,128)} %get-tuple-element.9.gain), custom_call_target="tpu_custom_call" | custom-call | tf_op jit(solution)/shard_map/pallas_call | solution.py:422

commit v3 on v2

--- a/solution.py
+++ b/solution.py
@@ -364,7 +364,7 @@
         copy.wait()
 
 
-PAIRS = 4
+PAIRS = 2
 
 
 def local(query_raw, key_raw, value_rows, out_cotangent, image_ids, owners, gains):

time: 40 us -> 41.1 us (1.028)
  Pallas kernels: 39.2 us -> 40.3 us
    pallas_call x1, Pallas kernels: 2.87 us -> 3.91 us  [local(): pl.pallas_call(place, out_shape=(grad, grad, grad, gain), in_specs=[hbm]...]
where the time goes in v3:
time: 41.1 us; the launch traced here: 41 us
  Pallas kernels  40.3 us (98%)
  between operations  0.64 us (2%)
    pallas_call x1, Pallas kernels, local(): pl.pallas_call(functools.partial(kernel, n, groups, pmax), out_shape=(jax...  36.4 us
    pallas_call x1, Pallas kernels, local(): pl.pallas_call(place, out_shape=(grad, grad, grad, gain), in_specs=[hbm]...  3.91 us

profile of v3, /device:TPU:0, one launch (start us, length us, event | category | flops | bytes accessed | tf_op | source)
XLA Modules:
  0.0 41.0 jit_solution(13818082194615292533)
XLA Ops:
  0.6 36.4 %shard_map.102 = (bf16[192,3072]{1,0:T(8,128)(2,1)}, bf16[128,192]{1,0:T(8,128)(2,1)}, f32[2,128]{1,0:T(2,128)}) custom-call(bf16[192,1024]{1,0:T(8,128)(2,1)} %q_hbm.1, bf16[192,1024]{1,0:T(8,128)(2,1)} %k_hbm.1, bf16[192,1024]{1,0:T(8,128)(2,1)} %v_hbm.1, bf16[192,1024]{1,0:T(8,128)(2,1)} %d_hbm.1, s32[1,192]{1,0:T(1,128)} %bitcast.1, ...), custom_call_target="tpu_custom_call" | custom-call | flops 1207959552 | bytes 2752512 | tf_op jit(solution)/shard_map/pallas_call | solution.py:382
  37.0 3.9 %shard_map.103 = (bf16[128,1024]{1,0:T(8,128)(2,1)}, bf16[128,1024]{1,0:T(8,128)(2,1)}, bf16[128,1024]{1,0:T(8,128)(2,1)}, f32[2,128]{1,0:T(2,128)}) custom-call(bf16[192,3072]{1,0:T(8,128)(2,1)} %get-tuple-element.7.recv_hbm, bf16[128,192]{1,0:T(8,128)(2,1)} %get-tuple-element.8.order_hbm, f32[2,128]{1,0:T(2,128)} %get-tuple-element.9.gain), custom_call_target="tpu_custom_call" | custom-call | tf_op jit(solution)/shard_map/pallas_call | solution.py:422
